TPU v7x, 512 devices: a whole 4x4x16 slice. The times are simulated.
512 devices in a mesh: energy: 64 (over y_hi, z, core), pair: 8 (over x, y_lo).
Axes of the slice: x: 4, y: 4 (y_hi: 2, y_lo: 2; y = y_hi * 2 + y_lo), z: 16, core: 2. Of those that a mesh axis runs over, the one named last changes fastest.
Arguments:
- g_less: bfloat16 [2, 4096, 8192], P(None, 'energy', 'pair'), may hold values from -6 to 6
- g_greater: bfloat16 [2, 4096, 8192], P(None, 'energy', 'pair'), may hold values from -6 to 6
- pair_slot: int32 [8, 1024], P('pair'), may hold values from 0 to 1023, each once within a row
Outputs:
- pol_less: bfloat16 [2, 4096, 8192], P(None, 'energy', 'pair')
- pol_greater: bfloat16 [2, 4096, 8192], P(None, 'energy', 'pair')
Inputs may be any that keep to these rules, and one draw needn't show every extreme that they name: Each row of pair_slot is a permutation of the slots; rows p and p xor 1 pair their elements as mirrors through equal entries.
All inputs are finite; a program needn't handle non-finite values.
Results may differ from a plain program's by a relative error of at most 0.011.
Values may be sent and summed in bfloat16 or wider, within the bound.
A program may use at most 64 MiB of HBM per device.

v0:
```python
import functools
import math

import jax
import jax.numpy as jnp
import ml_dtypes
import numpy as np
from jax import lax
from jax.experimental import pallas as pl
from jax.experimental.pallas import tpu as pltpu
from jax.sharding import PartitionSpec as P

NE = 4096
N0 = 64
EDEV = 64
OWNERS = 2 * EDEV
SLOTS = 1024
MINE = SLOTS // OWNERS
ROWS = 2 * MINE
K0 = 128
K1 = 64
LENGTH = 2 * NE
F32 = jnp.float32
BF16 = jnp.bfloat16
MESH = pl.DeviceIdType.MESH


def upper_lower(table):
    upper = table.astype(ml_dtypes.bfloat16)
    lower = (table - upper.astype(np.float64)).astype(ml_dtypes.bfloat16)
    return upper, lower


def cos_sin(rows, cols, period):
    angle = (np.arange(rows)[:, None] * np.arange(cols)[None, :] % period) * (2.0 * math.pi / period)
    return np.cos(angle), np.sin(angle)


def tables():
    lanes = lambda *parts: np.concatenate(parts, axis=1)
    both = lambda table: np.concatenate(upper_lower(table))
    straight = lambda part: np.kron(np.eye(2), part)
    crossed = lambda part: np.kron(np.eye(2)[::-1], part)
    c, s = cos_sin(K0, EDEV, K0)
    first = [lanes(*upper_lower(lanes(c, s))), lanes(*upper_lower(lanes(c, -s)))]
    c, s = cos_sin(N0, K1, K1)
    own = both(np.block([[straight(c), -straight(s)], [straight(s), straight(c)]]))
    far = both(np.block([[crossed(c), crossed(s)], [-crossed(s), crossed(c)]]))
    ahead = both(np.block([[straight(c), straight(s)], [-straight(s), straight(c)]]))
    behind = both(np.block([[crossed(c), crossed(s)], [crossed(s), -crossed(c)]]))
    c, s = cos_sin(EDEV, K0, K0)
    last = both(np.block([[c, -s], [s, c]]))
    coarse = np.concatenate(first + [own, far, ahead, behind, last])
    c, s = cos_sin(K0, N0, LENGTH)
    scale = 1.0 / (math.sqrt(NE) * LENGTH)
    fine = np.stack([lanes(c, c), lanes(s, s), lanes(s, s) * scale, -lanes(c, c) * scale])
    return coarse.reshape(-1, 128, 256).astype(np.float32), fine.astype(np.float32)


def dot(left, right, dims=((1,), (0,))):
    return lax.dot_general(left, right, (dims, ((), ())), preferred_element_type=F32)


def split(value):
    upper = value.astype(BF16)
    return upper, (value - upper.astype(F32)).astype(BF16)


def correlate(recv, send, coarse, fine, flat, y_own, y_far):
    first, own, far, ahead, behind, last = 0, 2, 6, 10, 14, 18
    flat[...] = recv[...].astype(F32).reshape(OWNERS * ROWS, 128)

    def line(side, part, slot):
        return pl.ds(side * ROWS + part * MINE + slot, EDEV, stride=2 * ROWS)

    def spectrum(side, slot, into):
        re, im = flat[line(side, 0, slot), :], flat[line(side, 1, slot), :]
        top = jnp.concatenate([re, im], axis=1).astype(BF16)
        bottom = jnp.concatenate([im, -re], axis=1).astype(BF16)
        step = dot(coarse[first + side], jnp.concatenate([top, bottom, top, bottom], axis=0))
        re, im = step[:, :128], step[:, 128:]
        c, s = fine[0], fine[1]
        if side == 0:
            re, im = re * c + im * s, im * c - re * s
        else:
            re, im = re * c - im * s, im * c + re * s
        into[pl.ds(slot * K0, K0), :] = jnp.concatenate(split(jnp.concatenate([re, im], axis=1)), axis=1)

    def forward(step, carry):
        for member in range(2):
            spectrum(0, step * 2 + member, y_own)
            spectrum(1, step * 2 + member, y_far)
        return carry

    lax.fori_loop(0, MINE // 2, forward, 0)

    def triple(value, table):
        upper = coarse[table : table + 2].reshape(256, 256)
        lower = coarse[table + 2 : table + 4].reshape(256, 256)
        return dot(
            jnp.concatenate([value, value[:, :256]], axis=1), jnp.concatenate([upper, upper, lower], axis=0)
        )

    group = 4

    def product(step, carry):
        rows = pl.ds(step * (group * K0), group * K0)
        left, right = triple(y_own[rows, :], own), triple(y_far[rows, :], far)
        a, b, c, d = left[:, :128], left[:, 128:], right[:, :128], right[:, 128:]
        spec = jnp.concatenate(split(jnp.concatenate([a * c - b * d, a * d + b * c], axis=1)), axis=1)
        lags = (triple(spec, ahead), triple(spec, behind))
        for member in range(group):
            tops, bottoms = [], []
            for part in lags:
                re, im = part[member * K0 : (member + 1) * K0, :128], part[member * K0 : (member + 1) * K0, 128:]
                tops.append(re * fine[2] - im * fine[3])
                bottoms.append(re * fine[3] + im * fine[2])
            upper, lower = split(
                jnp.concatenate([jnp.concatenate(tops, axis=1), jnp.concatenate(bottoms, axis=1)], axis=0)
            )
            result = dot(
                jnp.concatenate([coarse[last], coarse[last], coarse[last + 1]], axis=1),
                jnp.concatenate([upper, lower, upper], axis=0),
            )
            slot = step * group + member
            flat[line(0, 0, slot), :] = result[:EDEV, :128]
            flat[line(0, 1, slot), :] = result[EDEV:, :128]
            flat[line(1, 0, slot), :] = -result[:EDEV, 128:]
            flat[line(1, 1, slot), :] = result[EDEV:, 128:]
        return carry

    lax.fori_loop(0, MINE // group, product, 0)
    send[...] = flat[...].reshape(OWNERS, ROWS, 128).astype(BF16)


def one_hot(slot):
    order = lax.broadcasted_iota(jnp.int32, (SLOTS, SLOTS), 0)
    return jnp.where(order == slot, 1.0, 0.0).astype(BF16)


def kernel(
    less_hbm, greater_hbm, slot_hbm, coarse_hbm, fine_hbm,
    recv_two,
    less, greater, slot, wide, coarse, fine,
    hot, send_one, recv_one, send_two, flat, y_own, y_far,
    sent, came, kept, fetched,
):
    e = lax.axis_index("energy")
    p = lax.axis_index("pair")
    core, z, x = lax.rem(e, 2), lax.rem(lax.div(e, 2), 16), lax.div(p, 2)
    y = lax.div(e, 32) * 2 + lax.rem(p, 2)
    me = e * 2 + lax.rem(p, 2)

    sources = (slot_hbm, less_hbm, greater_hbm, coarse_hbm, fine_hbm)
    places = (slot, less, greater, wide, fine)
    fetches = [pltpu.make_async_copy(a, b, fetched.at[i]) for i, (a, b) in enumerate(zip(sources, places))]
    for fetch in fetches:
        fetch.start()

    columns = []
    for dy in range(4):
        to_y = lax.rem(y + dy, 4)
        columns.append((lax.div(to_y, 2) * 32, lax.rem(to_y, 2)))

    def every_peer(act):
        for to_core in (1, 0):

            def along_z(t, carry):
                dz = 8 + (1 - 2 * lax.rem(t, 2)) * lax.div(t + 1, 2)
                low = lax.rem(z + dz, 16) * 2 + to_core
                for dy, (high, side) in enumerate(columns):
                    run = functools.partial(act, high + low, x * 2 + side, (high + low) * 2 + side)
                    if dy == 0:
                        pl.when(jnp.logical_or(t < 15, core != to_core))(run)
                    else:
                        run()
                return carry

            lax.fori_loop(0, 16, along_z, 0)

    barrier = pltpu.get_barrier_semaphore()

    def greet(to_e, to_p, to):
        pl.semaphore_signal(barrier, inc=1, device_id=(to_e, to_p), device_id_type=MESH)

    every_peer(greet)

    fetches[0].wait()
    hot[...] = one_hot(slot[...])
    fetches[1].wait()
    fetches[2].wait()
    halves = []
    for part in range(2):
        value = jnp.concatenate([less[part], greater[part]], axis=0)
        halves.append(dot(hot[...], value, ((1,), (1,))).reshape(OWNERS, MINE, 128))
    send_one[...] = jnp.concatenate(halves, axis=1).astype(BF16)

    pl.semaphore_wait(barrier, OWNERS - 1)

    def exchange(source, target, at, meanwhile=None):
        def start(to_e, to_p, to):
            pltpu.make_async_remote_copy(
                src_ref=source.at[to],
                dst_ref=target.at[me],
                send_sem=sent.at[at],
                recv_sem=came.at[at],
                device_id=(to_e, to_p),
                device_id_type=MESH,
            ).start()

        every_peer(start)
        stay = pltpu.make_async_copy(source.at[me], target.at[me], kept)
        stay.start()
        stay.wait()
        if meanwhile is not None:
            meanwhile()
        others = pl.ds(0, OWNERS - 1)
        pltpu.make_async_copy(target.at[others], target.at[others], came.at[at]).wait()

    def drain(source, at):
        others = pl.ds(0, OWNERS - 1)
        pltpu.make_async_copy(source.at[others], source.at[others], sent.at[at]).wait()

    def narrow():
        fetches[3].wait()
        fetches[4].wait()
        coarse[...] = wide[...].astype(BF16)

    exchange(send_one, recv_one, 0, narrow)
    correlate(recv_one, send_two, coarse, fine, flat, y_own, y_far)
    exchange(send_two, recv_two, 1)

    drain(send_one, 0)
    drain(send_two, 1)


def reorder(back_hbm, slot_hbm, out_less, out_greater, back, slot, fetched):
    fetches = [
        pltpu.make_async_copy(slot_hbm, slot, fetched.at[0]),
        pltpu.make_async_copy(back_hbm, back, fetched.at[1]),
    ]
    for fetch in fetches:
        fetch.start()
    fetches[0].wait()
    hot = one_hot(slot[...])
    fetches[1].wait()
    value = back[...].astype(F32)
    for part in range(2):
        ordered = value[:, part * MINE : (part + 1) * MINE].reshape(SLOTS, 128).astype(BF16)
        result = dot(ordered, hot, ((0,), (0,))).astype(BF16)
        out_less[part] = result[:N0]
        out_greater[part] = result[N0:]


def per_device(g_less, g_greater, pair_slot):
    coarse, fine = tables()
    vmem, hbm = pl.BlockSpec(memory_space=pltpu.VMEM), pl.BlockSpec(memory_space=pltpu.HBM)
    grant = 60 * 1024 * 1024
    packets = pltpu.VMEM((OWNERS, ROWS, 128), BF16)
    back = pl.pallas_call(
        kernel,
        out_shape=jax.ShapeDtypeStruct((OWNERS, ROWS, 128), BF16),
        in_specs=[hbm] * 5,
        out_specs=hbm,
        scratch_shapes=[
            pltpu.VMEM((2, N0, SLOTS), BF16),
            pltpu.VMEM((2, N0, SLOTS), BF16),
            pltpu.VMEM((1, SLOTS), jnp.int32),
            pltpu.VMEM(coarse.shape, F32),
            pltpu.VMEM(coarse.shape, BF16),
            pltpu.VMEM(fine.shape, F32),
            pltpu.VMEM((SLOTS, SLOTS), BF16),
            packets,
            packets,
            packets,
            pltpu.VMEM((OWNERS * ROWS, 128), F32),
            pltpu.VMEM((MINE * K0, 512), BF16),
            pltpu.VMEM((MINE * K0, 512), BF16),
            pltpu.SemaphoreType.DMA((2,)),
            pltpu.SemaphoreType.DMA((2,)),
            pltpu.SemaphoreType.DMA,
            pltpu.SemaphoreType.DMA((5,)),
        ],
        compiler_params=pltpu.CompilerParams(collective_id=0, has_side_effects=True, vmem_limit_bytes=grant),
        cost_estimate=pl.CostEstimate(flops=4 * 10**9, bytes_accessed=4 * 10**6, transcendentals=0),
    )(g_less, g_greater, pair_slot, jnp.asarray(coarse), jnp.asarray(fine))
    shape = jax.ShapeDtypeStruct((2, N0, SLOTS), BF16)
    return pl.pallas_call(
        reorder,
        out_shape=(shape, shape),
        in_specs=[hbm, hbm],
        out_specs=(vmem, vmem),
        scratch_shapes=[packets, pltpu.VMEM((1, SLOTS), jnp.int32), pltpu.SemaphoreType.DMA((2,))],
        compiler_params=pltpu.CompilerParams(vmem_limit_bytes=grant),
        cost_estimate=pl.CostEstimate(flops=10**9, bytes_accessed=10**6, transcendentals=0),
    )(back, pair_slot)


def solution(mesh):
    placed = (P(None, "energy", "pair"), P(None, "energy", "pair"), P("pair", None))
    return jax.shard_map(
        per_device,
        mesh=mesh,
        in_specs=placed,
        out_specs=(P(None, "energy", "pair"), P(None, "energy", "pair")),
        check_vma=False,
    )
```

profile of v0, /device:TPU:6, one launch (start us, length us, event | category | flops | bytes accessed | tf_op | source)
XLA Modules:
  0.0 69.5 jit_solution(4757516714547314796)
XLA Ops:
  0.6 66.1 %shard_map.68.back_hbm = bf16[128,16,128]{2,1,0:T(8,128)(2,1)} custom-call(bf16[2,64,1024]{2,1,0:T(8,128)(2,1)} %less_hbm.1, bf16[2,64,1024]{2,1,0:T(8,128)(2,1)} %greater_hbm.1, s32[1,1024]{1,0:T(1,128)} %slot_hbm.3, f32[20,128,256]{2,1,0:T(8,128)} %constant.4.clone.coarse_hbm, f32[4,128,128]{2,1,0:T(8,128)} %constant.5.clone.fine_hbm), custom_call_target="tpu_custom_call" | custom-call | flops 4000000000 | bytes 4000000 | tf_op jit(solution)/shard_map/pallas_call | solution.py:260
  66.7 2.8 %shard_map.69 = (bf16[2,64,1024]{2,1,0:T(8,128)(2,1)}, bf16[2,64,1024]{2,1,0:T(8,128)(2,1)}) custom-call(bf16[128,16,128]{2,1,0:T(8,128)(2,1)} %shard_map.68.back_hbm, s32[1,1024]{1,0:T(1,128)} %slot_hbm.3), custom_call_target="tpu_custom_call" | custom-call | flops 1000000000 | bytes 1000000 | tf_op jit(solution)/shard_map/pallas_call | solution.py:288
where the time goes:
time: 69.7 us; the launch traced here: 69.5 us
  Pallas kernels  68.9 us (99%)
    pallas_call x1, Pallas kernels, per_device(): pl.pallas_call(kernel, out_shape=jax.ShapeDtypeStruct((OWNERS, ROWS, 128)...  66.1 us
    pallas_call x1, Pallas kernels, per_device(): pl.pallas_call(reorder, out_shape=(shape, shape), in_specs=[hbm, hbm], ou...  2.8 us

commit v1 on v0

--- a/solution.py
+++ b/solution.py
@@ -165,18 +165,21 @@
     def every_peer(act):
         for to_core in (1, 0):
 
-            def along_z(t, carry):
-                dz = 8 + (1 - 2 * lax.rem(t, 2)) * lax.div(t + 1, 2)
-                low = lax.rem(z + dz, 16) * 2 + to_core
-                for dy, (high, side) in enumerate(columns):
-                    run = functools.partial(act, high + low, x * 2 + side, (high + low) * 2 + side)
-                    if dy == 0:
-                        pl.when(jnp.logical_or(t < 15, core != to_core))(run)
-                    else:
-                        run()
+            def at(dz, columns):
+                to_z = jnp.where(z + dz >= 16, z + dz - 16, z + dz)
+                for high, side in columns:
+                    to_e = high + to_z * 2 + to_core
+                    act(to_e, x * 2 + side, to_e * 2 + side)
+
+            def both_ways(near, carry):
+                at(7 - near, columns)
+                at(9 + near, columns)
                 return carry
 
-            lax.fori_loop(0, 16, along_z, 0)
+            at(8, columns)
+            lax.fori_loop(0, 7, both_ways, 0)
+            at(0, columns[1:])
+            pl.when(core != to_core)(functools.partial(at, 0, columns[:1]))
 
     barrier = pltpu.get_barrier_semaphore()
 

time: 69.7 us -> 69.6 us (level)
  no operation moved by 1% of the time
where the time goes in v1:
time: 69.6 us; the launch traced here: 69.4 us
  Pallas kernels  68.8 us (99%)
    pallas_call x1, Pallas kernels, per_device(): pl.pallas_call(kernel, out_shape=jax.ShapeDtypeStruct((OWNERS, ROWS, 128)...  66 us
    pallas_call x1, Pallas kernels, per_device(): pl.pallas_call(reorder, out_shape=(shape, shape), in_specs=[hbm, hbm], ou...  2.8 us

profile of v1, /device:TPU:6, one launch (start us, length us, event | category | flops | bytes accessed | tf_op | source)
XLA Modules:
  0.0 69.4 jit_solution(3335156877359040615)
XLA Ops:
  0.6 66.0 %shard_map.68.back_hbm = bf16[128,16,128]{2,1,0:T(8,128)(2,1)} custom-call(bf16[2,64,1024]{2,1,0:T(8,128)(2,1)} %less_hbm.1, bf16[2,64,1024]{2,1,0:T(8,128)(2,1)} %greater_hbm.1, s32[1,1024]{1,0:T(1,128)} %slot_hbm.3, f32[20,128,256]{2,1,0:T(8,128)} %constant.4.clone.coarse_hbm, f32[4,128,128]{2,1,0:T(8,128)} %constant.5.clone.fine_hbm), custom_call_target="tpu_custom_call" | custom-call | flops 4000000000 | bytes 4000000 | tf_op jit(solution)/shard_map/pallas_call | solution.py:263
  66.7 2.8 %shard_map.69 = (bf16[2,64,1024]{2,1,0:T(8,128)(2,1)}, bf16[2,64,1024]{2,1,0:T(8,128)(2,1)}) custom-call(bf16[128,16,128]{2,1,0:T(8,128)(2,1)} %shard_map.68.back_hbm, s32[1,1024]{1,0:T(1,128)} %slot_hbm.3), custom_call_target="tpu_custom_call" | custom-call | flops 1000000000 | bytes 1000000 | tf_op jit(solution)/shard_map/pallas_call | solution.py:291

commit v2 on v0

--- a/solution.py
+++ b/solution.py
@@ -133,8 +133,8 @@
     send[...] = flat[...].reshape(OWNERS, ROWS, 128).astype(BF16)
 
 
-def one_hot(slot):
-    order = lax.broadcasted_iota(jnp.int32, (SLOTS, SLOTS), 0)
+def one_hot(slot, begin, rows):
+    order = lax.broadcasted_iota(jnp.int32, (rows, SLOTS), 0) + begin
     return jnp.where(order == slot, 1.0, 0.0).astype(BF16)
 
 
@@ -148,8 +148,10 @@
     e = lax.axis_index("energy")
     p = lax.axis_index("pair")
     core, z, x = lax.rem(e, 2), lax.rem(lax.div(e, 2), 16), lax.div(p, 2)
-    y = lax.div(e, 32) * 2 + lax.rem(p, 2)
-    me = e * 2 + lax.rem(p, 2)
+    side = lax.rem(p, 2)
+    y = lax.div(e, 32) * 2 + side
+    place = e * 2 + side
+    owner = (1 - core) * EDEV + lax.div(e, 2) * 2 + side
 
     sources = (slot_hbm, less_hbm, greater_hbm, coarse_hbm, fine_hbm)
     places = (slot, less, greater, wide, fine)
@@ -160,81 +162,108 @@
     columns = []
     for dy in range(4):
         to_y = lax.rem(y + dy, 4)
-        columns.append((lax.div(to_y, 2) * 32, lax.rem(to_y, 2)))
-
-    def every_peer(act):
-        for to_core in (1, 0):
-
-            def along_z(t, carry):
-                dz = 8 + (1 - 2 * lax.rem(t, 2)) * lax.div(t + 1, 2)
-                low = lax.rem(z + dz, 16) * 2 + to_core
-                for dy, (high, side) in enumerate(columns):
-                    run = functools.partial(act, high + low, x * 2 + side, (high + low) * 2 + side)
-                    if dy == 0:
-                        pl.when(jnp.logical_or(t < 15, core != to_core))(run)
-                    else:
-                        run()
-                return carry
-
-            lax.fori_loop(0, 16, along_z, 0)
+        columns.append((lax.div(to_y, 2) * 16, lax.rem(to_y, 2)))
+
+    def at(dz, to_core, columns, act):
+        to_z = jnp.where(z + dz >= 16, z + dz - 16, z + dz)
+        for high, to_side in columns:
+            chip = high + to_z
+            act(
+                chip * 2 + to_core,
+                x * 2 + to_side,
+                (chip * 2 + to_core) * 2 + to_side,
+                (1 - to_core) * EDEV + chip * 2 + to_side,
+            )
+
+    def peers(cores, act):
+        def both_ways(near, carry):
+            for to_core in cores:
+                at(7 - near, to_core, columns, act)
+                at(9 + near, to_core, columns, act)
+            return carry
+
+        for to_core in cores:
+            at(8, to_core, columns, act)
+        lax.fori_loop(0, 7, both_ways, 0)
+        for to_core in cores:
+            at(0, to_core, columns[1:], act)
+            pl.when(core != to_core)(functools.partial(at, 0, to_core, columns[:1], act))
+
+    def some_peers(to_core, odd, act):
+        even = 1 - lax.rem(odd + z, 2)
+
+        def both_ways(near, carry):
+            at(7 + even - 2 * near, to_core, columns, act)
+            at(9 + even + 2 * near, to_core, columns, act)
+            return carry
+
+        lax.fori_loop(0, 3, both_ways, 0)
+        at(1 + even, to_core, columns, act)
+        at(15 + even, to_core, columns[1:], act)
+        pl.when(jnp.logical_or(even == 0, core != to_core))(
+            functools.partial(at, 15 + even, to_core, columns[:1], act)
+        )
 
     barrier = pltpu.get_barrier_semaphore()
 
-    def greet(to_e, to_p, to):
+    def greet(to_e, to_p, to_place, to_owner):
         pl.semaphore_signal(barrier, inc=1, device_id=(to_e, to_p), device_id_type=MESH)
 
-    every_peer(greet)
-
+    peers((1, 0), greet)
     fetches[0].wait()
-    hot[...] = one_hot(slot[...])
+    hot[...] = one_hot(slot[...], 0, SLOTS)
+
+    def remote(src, dst, turn, to_e, to_p):
+        pltpu.make_async_remote_copy(
+            src_ref=src,
+            dst_ref=dst,
+            send_sem=sent.at[turn],
+            recv_sem=came.at[turn],
+            device_id=(to_e, to_p),
+            device_id_type=MESH,
+        ).start()
+
+    def out(to_e, to_p, to_place, to_owner):
+        remote(send_one.at[to_owner], recv_one.at[place], 0, to_e, to_p)
+
+    def back(to_e, to_p, to_place, to_owner):
+        remote(send_two.at[to_place], recv_two.at[owner], 1, to_e, to_p)
+
+    others = pl.ds(0, OWNERS - 1)
+
+    def arrive(src, dst, target, turn):
+        stay = pltpu.make_async_copy(src, dst, kept)
+        stay.start()
+        stay.wait()
+        pltpu.make_async_copy(target.at[others], target.at[others], came.at[turn]).wait()
+
     fetches[1].wait()
     fetches[2].wait()
-    halves = []
-    for part in range(2):
-        value = jnp.concatenate([less[part], greater[part]], axis=0)
-        halves.append(dot(hot[...], value, ((1,), (1,))).reshape(OWNERS, MINE, 128))
-    send_one[...] = jnp.concatenate(halves, axis=1).astype(BF16)
-
-    pl.semaphore_wait(barrier, OWNERS - 1)
-
-    def exchange(source, target, at, meanwhile=None):
-        def start(to_e, to_p, to):
-            pltpu.make_async_remote_copy(
-                src_ref=source.at[to],
-                dst_ref=target.at[me],
-                send_sem=sent.at[at],
-                recv_sem=came.at[at],
-                device_id=(to_e, to_p),
-                device_id_type=MESH,
-            ).start()
-
-        every_peer(start)
-        stay = pltpu.make_async_copy(source.at[me], target.at[me], kept)
-        stay.start()
-        stay.wait()
-        if meanwhile is not None:
-            meanwhile()
-        others = pl.ds(0, OWNERS - 1)
-        pltpu.make_async_copy(target.at[others], target.at[others], came.at[at]).wait()
-
-    def drain(source, at):
-        others = pl.ds(0, OWNERS - 1)
-        pltpu.make_async_copy(source.at[others], source.at[others], sent.at[at]).wait()
-
-    def narrow():
-        fetches[3].wait()
-        fetches[4].wait()
-        coarse[...] = wide[...].astype(BF16)
-
-    exchange(send_one, recv_one, 0, narrow)
+    value = jnp.concatenate([less[0], greater[0], less[1], greater[1]], axis=0)
+    for to_core in (1, 0):
+        half = SLOTS // 2
+        ordered = dot(hot[(1 - to_core) * half : (2 - to_core) * half, :], value, ((1,), (1,)))
+        parts = [ordered[:, part * 128 : (part + 1) * 128].reshape(EDEV, MINE, 128) for part in range(2)]
+        send_one[(1 - to_core) * EDEV : (2 - to_core) * EDEV] = jnp.concatenate(parts, axis=1).astype(BF16)
+        if to_core == 1:
+            pl.semaphore_wait(barrier, OWNERS - 1)
+        for odd in (1, 0):
+            some_peers(to_core, odd, out)
+
+    fetches[3].wait()
+    fetches[4].wait()
+    coarse[...] = wide[...].astype(BF16)
+    arrive(send_one.at[owner], recv_one.at[place], recv_one, 0)
     correlate(recv_one, send_two, coarse, fine, flat, y_own, y_far)
-    exchange(send_two, recv_two, 1)
-
-    drain(send_one, 0)
-    drain(send_two, 1)
-
-
-def reorder(back_hbm, slot_hbm, out_less, out_greater, back, slot, fetched):
+    for to_core in (1, 0):
+        peers((to_core,), back)
+    arrive(send_two.at[place], recv_two.at[owner], recv_two, 1)
+
+    for turn, source in enumerate((send_one, send_two)):
+        pltpu.make_async_copy(source.at[others], source.at[others], sent.at[turn]).wait()
+
+
+def reorder(back_hbm, slot_hbm, less_hbm, greater_hbm, back, slot, less, greater, fetched, stored):
     fetches = [
         pltpu.make_async_copy(slot_hbm, slot, fetched.at[0]),
         pltpu.make_async_copy(back_hbm, back, fetched.at[1]),
@@ -242,19 +271,26 @@
     for fetch in fetches:
         fetch.start()
     fetches[0].wait()
-    hot = one_hot(slot[...])
+    hot = one_hot(slot[...], 0, SLOTS)
     fetches[1].wait()
     value = back[...].astype(F32)
+    ordered = jnp.concatenate(
+        [value[:, part * MINE : (part + 1) * MINE].reshape(SLOTS, 128) for part in range(2)], axis=1
+    )
+    result = dot(ordered.astype(BF16), hot, ((0,), (0,))).astype(BF16)
+    stores = []
     for part in range(2):
-        ordered = value[:, part * MINE : (part + 1) * MINE].reshape(SLOTS, 128).astype(BF16)
-        result = dot(ordered, hot, ((0,), (0,))).astype(BF16)
-        out_less[part] = result[:N0]
-        out_greater[part] = result[N0:]
+        for array, (kept, result_hbm) in enumerate(((less, less_hbm), (greater, greater_hbm))):
+            kept[part] = result[(part * 2 + array) * N0 : (part * 2 + array + 1) * N0]
+            stores.append(pltpu.make_async_copy(kept.at[part], result_hbm.at[part], stored.at[part, array]))
+            stores[-1].start()
+    for store in stores:
+        store.wait()
 
 
 def per_device(g_less, g_greater, pair_slot):
     coarse, fine = tables()
-    vmem, hbm = pl.BlockSpec(memory_space=pltpu.VMEM), pl.BlockSpec(memory_space=pltpu.HBM)
+    hbm = pl.BlockSpec(memory_space=pltpu.HBM)
     grant = 60 * 1024 * 1024
     packets = pltpu.VMEM((OWNERS, ROWS, 128), BF16)
     back = pl.pallas_call(
@@ -289,8 +325,15 @@
         reorder,
         out_shape=(shape, shape),
         in_specs=[hbm, hbm],
-        out_specs=(vmem, vmem),
-        scratch_shapes=[packets, pltpu.VMEM((1, SLOTS), jnp.int32), pltpu.SemaphoreType.DMA((2,))],
+        out_specs=(hbm, hbm),
+        scratch_shapes=[
+            packets,
+            pltpu.VMEM((1, SLOTS), jnp.int32),
+            pltpu.VMEM(shape.shape, BF16),
+            pltpu.VMEM(shape.shape, BF16),
+            pltpu.SemaphoreType.DMA((2,)),
+            pltpu.SemaphoreType.DMA((2, 2)),
+        ],
         compiler_params=pltpu.CompilerParams(vmem_limit_bytes=grant),
         cost_estimate=pl.CostEstimate(flops=10**9, bytes_accessed=10**6, transcendentals=0),
     )(back, pair_slot)

time: 69.7 us -> 69.4 us (level)
  no operation moved by 1% of the time
where the time goes in v2:
time: 69.4 us; the launch traced here: 69.2 us
  Pallas kernels  68.6 us (99%)
    pallas_call x1, Pallas kernels, per_device(): pl.pallas_call(kernel, out_shape=jax.ShapeDtypeStruct((OWNERS, ROWS, 128)...  65.8 us
    pallas_call x1, Pallas kernels, per_device(): pl.pallas_call(reorder, out_shape=(shape, shape), in_specs=[hbm, hbm], ou...  2.78 us

profile of v2, /device:TPU:6, one launch (start us, length us, event | category | flops | bytes accessed | tf_op | source)
XLA Modules:
  0.0 69.2 jit_solution(4292999517401025267)
XLA Ops:
  0.6 65.8 %shard_map.68.back_hbm = bf16[128,16,128]{2,1,0:T(8,128)(2,1)} custom-call(bf16[2,64,1024]{2,1,0:T(8,128)(2,1)} %less_hbm.1, bf16[2,64,1024]{2,1,0:T(8,128)(2,1)} %greater_hbm.1, s32[1,1024]{1,0:T(1,128)} %slot_hbm.3, f32[20,128,256]{2,1,0:T(8,128)} %constant.4.clone.coarse_hbm, f32[4,128,128]{2,1,0:T(8,128)} %constant.5.clone.fine_hbm), custom_call_target="tpu_custom_call" | custom-call | flops 4000000000 | bytes 4000000 | tf_op jit(solution)/shard_map/pallas_call | solution.py:296
  66.4 2.8 %shard_map.69 = (bf16[2,64,1024]{2,1,0:T(8,128)(2,1)}, bf16[2,64,1024]{2,1,0:T(8,128)(2,1)}) custom-call(bf16[128,16,128]{2,1,0:T(8,128)(2,1)} %shard_map.68.back_hbm, s32[1,1024]{1,0:T(1,128)} %slot_hbm.3), custom_call_target="tpu_custom_call" | custom-call | flops 1000000000 | bytes 1000000 | tf_op jit(solution)/shard_map/pallas_call | solution.py:324

commit v3 on v2

--- a/solution.py
+++ b/solution.py
@@ -86,13 +86,9 @@
             re, im = re * c - im * s, im * c + re * s
         into[pl.ds(slot * K0, K0), :] = jnp.concatenate(split(jnp.concatenate([re, im], axis=1)), axis=1)
 
-    def forward(step, carry):
-        for member in range(2):
-            spectrum(0, step * 2 + member, y_own)
-            spectrum(1, step * 2 + member, y_far)
-        return carry
-
-    lax.fori_loop(0, MINE // 2, forward, 0)
+    for slot in range(MINE):
+        spectrum(0, slot, y_own)
+        spectrum(1, slot, y_far)
 
     def triple(value, table):
         upper = coarse[table : table + 2].reshape(256, 256)
@@ -102,8 +98,7 @@
         )
 
     group = 4
-
-    def product(step, carry):
+    for step in range(MINE // group):
         rows = pl.ds(step * (group * K0), group * K0)
         left, right = triple(y_own[rows, :], own), triple(y_far[rows, :], far)
         a, b, c, d = left[:, :128], left[:, 128:], right[:, :128], right[:, 128:]
@@ -118,18 +113,14 @@
             upper, lower = split(
                 jnp.concatenate([jnp.concatenate(tops, axis=1), jnp.concatenate(bottoms, axis=1)], axis=0)
             )
-            result = dot(
-                jnp.concatenate([coarse[last], coarse[last], coarse[last + 1]], axis=1),
-                jnp.concatenate([upper, lower, upper], axis=0),
-            )
+            both = dot(coarse[last : last + 2].reshape(256, 256), upper)
+            result = both[:128] + both[128:] + dot(coarse[last], lower)
             slot = step * group + member
             flat[line(0, 0, slot), :] = result[:EDEV, :128]
             flat[line(0, 1, slot), :] = result[EDEV:, :128]
             flat[line(1, 0, slot), :] = -result[:EDEV, 128:]
             flat[line(1, 1, slot), :] = result[EDEV:, 128:]
-        return carry
-
-    lax.fori_loop(0, MINE // group, product, 0)
+
     send[...] = flat[...].reshape(OWNERS, ROWS, 128).astype(BF16)
 
 

time: 69.4 us -> 68.7 us (0.990)
  Pallas kernels: 68.6 us -> 67.9 us
where the time goes in v3:
time: 68.7 us; the launch traced here: 68.6 us
  Pallas kernels  67.9 us (99%)
    pallas_call x1, Pallas kernels, per_device(): pl.pallas_call(kernel, out_shape=jax.ShapeDtypeStruct((OWNERS, ROWS, 128)...  65.2 us
    pallas_call x1, Pallas kernels, per_device(): pl.pallas_call(reorder, out_shape=(shape, shape), in_specs=[hbm, hbm], ou...  2.77 us

profile of v3, /device:TPU:6, one launch (start us, length us, event | category | flops | bytes accessed | tf_op | source)
XLA Modules:
  0.0 68.6 jit_solution(2859334551570060870)
XLA Ops:
  0.6 65.2 %shard_map.68.back_hbm = bf16[128,16,128]{2,1,0:T(8,128)(2,1)} custom-call(bf16[2,64,1024]{2,1,0:T(8,128)(2,1)} %less_hbm.1, bf16[2,64,1024]{2,1,0:T(8,128)(2,1)} %greater_hbm.1, s32[1,1024]{1,0:T(1,128)} %slot_hbm.3, f32[20,128,256]{2,1,0:T(8,128)} %constant.4.clone.coarse_hbm, f32[4,128,128]{2,1,0:T(8,128)} %constant.5.clone.fine_hbm), custom_call_target="tpu_custom_call" | custom-call | flops 4000000000 | bytes 4000000 | tf_op jit(solution)/shard_map/pallas_call | solution.py:287
  65.8 2.8 %shard_map.69 = (bf16[2,64,1024]{2,1,0:T(8,128)(2,1)}, bf16[2,64,1024]{2,1,0:T(8,128)(2,1)}) custom-call(bf16[128,16,128]{2,1,0:T(8,128)(2,1)} %shard_map.68.back_hbm, s32[1,1024]{1,0:T(1,128)} %slot_hbm.3), custom_call_target="tpu_custom_call" | custom-call | flops 1000000000 | bytes 1000000 | tf_op jit(solution)/shard_map/pallas_call | solution.py:315

commit v4 on v3

--- a/solution.py
+++ b/solution.py
@@ -17,6 +17,7 @@
 SLOTS = 1024
 MINE = SLOTS // OWNERS
 ROWS = 2 * MINE
+EARLY_Z = 2
 K0 = 128
 K1 = 64
 LENGTH = 2 * NE
@@ -155,8 +156,7 @@
         to_y = lax.rem(y + dy, 4)
         columns.append((lax.div(to_y, 2) * 16, lax.rem(to_y, 2)))
 
-    def at(dz, to_core, columns, act):
-        to_z = jnp.where(z + dz >= 16, z + dz - 16, z + dz)
+    def at_z(to_z, to_core, columns, act):
         for high, to_side in columns:
             chip = high + to_z
             act(
@@ -166,19 +166,22 @@
                 (1 - to_core) * EDEV + chip * 2 + to_side,
             )
 
-    def peers(cores, act):
+    def at(dz, to_core, columns, act):
+        at_z(jnp.where(z + dz >= 16, z + dz - 16, z + dz), to_core, columns, act)
+
+    def peers(cores, act, visit=at):
         def both_ways(near, carry):
             for to_core in cores:
-                at(7 - near, to_core, columns, act)
-                at(9 + near, to_core, columns, act)
+                visit(7 - near, to_core, columns, act)
+                visit(9 + near, to_core, columns, act)
             return carry
 
         for to_core in cores:
-            at(8, to_core, columns, act)
+            visit(8, to_core, columns, act)
         lax.fori_loop(0, 7, both_ways, 0)
         for to_core in cores:
-            at(0, to_core, columns[1:], act)
-            pl.when(core != to_core)(functools.partial(at, 0, to_core, columns[:1], act))
+            visit(0, to_core, columns[1:], act)
+            pl.when(core != to_core)(functools.partial(visit, 0, to_core, columns[:1], act))
 
     def some_peers(to_core, odd, act):
         even = 1 - lax.rem(odd + z, 2)
@@ -246,8 +249,16 @@
     coarse[...] = wide[...].astype(BF16)
     arrive(send_one.at[owner], recv_one.at[place], recv_one, 0)
     correlate(recv_one, send_two, coarse, fine, flat, y_own, y_far)
-    for to_core in (1, 0):
-        peers((to_core,), back)
+    peers((1,), back)
+    for to_z in range(EARLY_Z):
+        at_z(to_z, 0, columns[1:], back)
+        pl.when(jnp.logical_or(z != to_z, core != 0))(functools.partial(at_z, to_z, 0, columns[:1], back))
+
+    def later(dz, to_core, columns, act):
+        to_z = jnp.where(z + dz >= 16, z + dz - 16, z + dz)
+        pl.when(to_z >= EARLY_Z)(functools.partial(at_z, to_z, to_core, columns, act))
+
+    peers((0,), back, later)
     arrive(send_two.at[place], recv_two.at[owner], recv_two, 1)
 
     for turn, source in enumerate((send_one, send_two)):

time: 68.7 us -> 68.1 us (level)
  no operation moved by 1% of the time
where the time goes in v4:
time: 68.1 us; the launch traced here: 68 us
  Pallas kernels  67.3 us (99%)
    pallas_call x1, Pallas kernels, per_device(): pl.pallas_call(kernel, out_shape=jax.ShapeDtypeStruct((OWNERS, ROWS, 128)...  64.6 us
    pallas_call x1, Pallas kernels, per_device(): pl.pallas_call(reorder, out_shape=(shape, shape), in_specs=[hbm, hbm], ou...  2.77 us

profile of v4, /device:TPU:6, one launch (start us, length us, event | category | flops | bytes accessed | tf_op | source)
XLA Modules:
  0.0 68.0 jit_solution(16780285193753201081)
XLA Ops:
  0.6 64.6 %shard_map.68.back_hbm = bf16[128,16,128]{2,1,0:T(8,128)(2,1)} custom-call(bf16[2,64,1024]{2,1,0:T(8,128)(2,1)} %less_hbm.1, bf16[2,64,1024]{2,1,0:T(8,128)(2,1)} %greater_hbm.1, s32[1,1024]{1,0:T(1,128)} %slot_hbm.3, f32[20,128,256]{2,1,0:T(8,128)} %constant.4.clone.coarse_hbm, f32[4,128,128]{2,1,0:T(8,128)} %constant.5.clone.fine_hbm), custom_call_target="tpu_custom_call" | custom-call | flops 4000000000 | bytes 4000000 | tf_op jit(solution)/shard_map/pallas_call | solution.py:298
  65.2 2.8 %shard_map.69 = (bf16[2,64,1024]{2,1,0:T(8,128)(2,1)}, bf16[2,64,1024]{2,1,0:T(8,128)(2,1)}) custom-call(bf16[128,16,128]{2,1,0:T(8,128)(2,1)} %shard_map.68.back_hbm, s32[1,1024]{1,0:T(1,128)} %slot_hbm.3), custom_call_target="tpu_custom_call" | custom-call | flops 1000000000 | bytes 1000000 | tf_op jit(solution)/shard_map/pallas_call | solution.py:326

commit v5 on v4

--- a/solution.py
+++ b/solution.py
@@ -172,8 +172,9 @@
     def peers(cores, act, visit=at):
         def both_ways(near, carry):
             for to_core in cores:
-                visit(7 - near, to_core, columns, act)
-                visit(9 + near, to_core, columns, act)
+                for column in columns:
+                    visit(7 - near, to_core, [column], act)
+                    visit(9 + near, to_core, [column], act)
             return carry
 
         for to_core in cores:
@@ -187,13 +188,16 @@
         even = 1 - lax.rem(odd + z, 2)
 
         def both_ways(near, carry):
-            at(7 + even - 2 * near, to_core, columns, act)
-            at(9 + even + 2 * near, to_core, columns, act)
+            for column in columns:
+                at(7 + even - 2 * near, to_core, [column], act)
+                at(9 + even + 2 * near, to_core, [column], act)
             return carry
 
         lax.fori_loop(0, 3, both_ways, 0)
-        at(1 + even, to_core, columns, act)
-        at(15 + even, to_core, columns[1:], act)
+        at(1 + even, to_core, columns[:1], act)
+        for column in columns[1:]:
+            at(1 + even, to_core, [column], act)
+            at(15 + even, to_core, [column], act)
         pl.when(jnp.logical_or(even == 0, core != to_core))(
             functools.partial(at, 15 + even, to_core, columns[:1], act)
         )
@@ -249,10 +253,10 @@
     coarse[...] = wide[...].astype(BF16)
     arrive(send_one.at[owner], recv_one.at[place], recv_one, 0)
     correlate(recv_one, send_two, coarse, fine, flat, y_own, y_far)
-    peers((1,), back)
     for to_z in range(EARLY_Z):
         at_z(to_z, 0, columns[1:], back)
         pl.when(jnp.logical_or(z != to_z, core != 0))(functools.partial(at_z, to_z, 0, columns[:1], back))
+    peers((1,), back)
 
     def later(dz, to_core, columns, act):
         to_z = jnp.where(z + dz >= 16, z + dz - 16, z + dz)

time: 68.1 us -> 68 us (level)
  the two profiles are of different devices: /device:TPU:6 before, /device:TPU:70 now
where the time goes in v5:
time: 68 us; the launch traced here: 67.9 us
  Pallas kernels  67.3 us (99%)
    pallas_call x1, Pallas kernels, per_device(): pl.pallas_call(kernel, out_shape=jax.ShapeDtypeStruct((OWNERS, ROWS, 128)...  64.5 us
    pallas_call x1, Pallas kernels, per_device(): pl.pallas_call(reorder, out_shape=(shape, shape), in_specs=[hbm, hbm], ou...  2.77 us

profile of v5, /device:TPU:70, one launch (start us, length us, event | category | flops | bytes accessed | tf_op | source)
XLA Modules:
  0.0 67.9 jit_solution(9807245496878181765)
XLA Ops:
  0.6 64.5 %shard_map.68.back_hbm = bf16[128,16,128]{2,1,0:T(8,128)(2,1)} custom-call(bf16[2,64,1024]{2,1,0:T(8,128)(2,1)} %less_hbm.1, bf16[2,64,1024]{2,1,0:T(8,128)(2,1)} %greater_hbm.1, s32[1,1024]{1,0:T(1,128)} %slot_hbm.3, f32[20,128,256]{2,1,0:T(8,128)} %constant.4.clone.coarse_hbm, f32[4,128,128]{2,1,0:T(8,128)} %constant.5.clone.fine_hbm), custom_call_target="tpu_custom_call" | custom-call | flops 4000000000 | bytes 4000000 | tf_op jit(solution)/shard_map/pallas_call | solution.py:302
  65.1 2.8 %shard_map.69 = (bf16[2,64,1024]{2,1,0:T(8,128)(2,1)}, bf16[2,64,1024]{2,1,0:T(8,128)(2,1)}) custom-call(bf16[128,16,128]{2,1,0:T(8,128)(2,1)} %shard_map.68.back_hbm, s32[1,1024]{1,0:T(1,128)} %slot_hbm.3), custom_call_target="tpu_custom_call" | custom-call | flops 1000000000 | bytes 1000000 | tf_op jit(solution)/shard_map/pallas_call | solution.py:330

commit v6 on v3

--- a/solution.py
+++ b/solution.py
@@ -15,7 +15,8 @@
 EDEV = 64
 OWNERS = 2 * EDEV
 SLOTS = 1024
-MINE = SLOTS // OWNERS
+ROUNDS = 2
+MINE = SLOTS // OWNERS // ROUNDS
 ROWS = 2 * MINE
 K0 = 128
 K1 = 64
@@ -97,7 +98,7 @@
             jnp.concatenate([value, value[:, :256]], axis=1), jnp.concatenate([upper, upper, lower], axis=0)
         )
 
-    group = 4
+    group = MINE
     for step in range(MINE // group):
         rows = pl.ds(step * (group * K0), group * K0)
         left, right = triple(y_own[rows, :], own), triple(y_far[rows, :], far)
@@ -124,16 +125,18 @@
     send[...] = flat[...].reshape(OWNERS, ROWS, 128).astype(BF16)
 
 
-def one_hot(slot, begin, rows):
-    order = lax.broadcasted_iota(jnp.int32, (rows, SLOTS), 0) + begin
-    return jnp.where(order == slot, 1.0, 0.0).astype(BF16)
+def one_hot(slot, rounds):
+    owners = (len(rounds) * OWNERS, SLOTS)
+    first = (lax.broadcasted_iota(jnp.int32, owners, 0) + rounds[0] * OWNERS) * MINE
+    hits = [jnp.where(first == slot - mine, 1.0, 0.0) for mine in range(MINE)]
+    return jnp.concatenate(hits, axis=0).astype(BF16)
 
 
 def kernel(
     less_hbm, greater_hbm, slot_hbm, coarse_hbm, fine_hbm,
     recv_two,
     less, greater, slot, wide, coarse, fine,
-    hot, send_one, recv_one, send_two, flat, y_own, y_far,
+    send_one, recv_one, send_two, flat, y_own, y_far,
     sent, came, kept, fetched,
 ):
     e = lax.axis_index("energy")
@@ -141,8 +144,7 @@
     core, z, x = lax.rem(e, 2), lax.rem(lax.div(e, 2), 16), lax.div(p, 2)
     side = lax.rem(p, 2)
     y = lax.div(e, 32) * 2 + side
-    place = e * 2 + side
-    owner = (1 - core) * EDEV + lax.div(e, 2) * 2 + side
+    me = e * 2 + side
 
     sources = (slot_hbm, less_hbm, greater_hbm, coarse_hbm, fine_hbm)
     places = (slot, less, greater, wide, fine)
@@ -155,106 +157,89 @@
         to_y = lax.rem(y + dy, 4)
         columns.append((lax.div(to_y, 2) * 16, lax.rem(to_y, 2)))
 
-    def at(dz, to_core, columns, act):
-        to_z = jnp.where(z + dz >= 16, z + dz - 16, z + dz)
-        for high, to_side in columns:
-            chip = high + to_z
-            act(
-                chip * 2 + to_core,
-                x * 2 + to_side,
-                (chip * 2 + to_core) * 2 + to_side,
-                (1 - to_core) * EDEV + chip * 2 + to_side,
-            )
-
-    def peers(cores, act):
+    def peers(act):
+        def at(dz, to_core, columns):
+            to_z = jnp.where(z + dz >= 16, z + dz - 16, z + dz)
+            for high, to_side in columns:
+                to_e = (high + to_z) * 2 + to_core
+                act(to_e, x * 2 + to_side, to_e * 2 + to_side)
+
         def both_ways(near, carry):
-            for to_core in cores:
-                at(7 - near, to_core, columns, act)
-                at(9 + near, to_core, columns, act)
+            for to_core in (1, 0):
+                at(7 - near, to_core, columns)
+                at(9 + near, to_core, columns)
             return carry
 
-        for to_core in cores:
-            at(8, to_core, columns, act)
+        for to_core in (1, 0):
+            at(8, to_core, columns)
         lax.fori_loop(0, 7, both_ways, 0)
-        for to_core in cores:
-            at(0, to_core, columns[1:], act)
-            pl.when(core != to_core)(functools.partial(at, 0, to_core, columns[:1], act))
-
-    def some_peers(to_core, odd, act):
-        even = 1 - lax.rem(odd + z, 2)
-
-        def both_ways(near, carry):
-            at(7 + even - 2 * near, to_core, columns, act)
-            at(9 + even + 2 * near, to_core, columns, act)
-            return carry
-
-        lax.fori_loop(0, 3, both_ways, 0)
-        at(1 + even, to_core, columns, act)
-        at(15 + even, to_core, columns[1:], act)
-        pl.when(jnp.logical_or(even == 0, core != to_core))(
-            functools.partial(at, 15 + even, to_core, columns[:1], act)
-        )
+        for to_core in (1, 0):
+            at(0, to_core, columns[1:])
+            pl.when(core != to_core)(functools.partial(at, 0, to_core, columns[:1]))
 
     barrier = pltpu.get_barrier_semaphore()
 
-    def greet(to_e, to_p, to_place, to_owner):
+    def greet(to_e, to_p, to):
         pl.semaphore_signal(barrier, inc=1, device_id=(to_e, to_p), device_id_type=MESH)
 
-    peers((1, 0), greet)
-    fetches[0].wait()
-    hot[...] = one_hot(slot[...], 0, SLOTS)
-
-    def remote(src, dst, turn, to_e, to_p):
-        pltpu.make_async_remote_copy(
-            src_ref=src,
-            dst_ref=dst,
-            send_sem=sent.at[turn],
-            recv_sem=came.at[turn],
-            device_id=(to_e, to_p),
-            device_id_type=MESH,
-        ).start()
-
-    def out(to_e, to_p, to_place, to_owner):
-        remote(send_one.at[to_owner], recv_one.at[place], 0, to_e, to_p)
-
-    def back(to_e, to_p, to_place, to_owner):
-        remote(send_two.at[to_place], recv_two.at[owner], 1, to_e, to_p)
+    peers(greet)
 
     others = pl.ds(0, OWNERS - 1)
 
-    def arrive(src, dst, target, turn):
-        stay = pltpu.make_async_copy(src, dst, kept)
+    def depart(source, target, turn, part):
+        def start(to_e, to_p, to):
+            pltpu.make_async_remote_copy(
+                src_ref=source.at[to],
+                dst_ref=target.at[me],
+                send_sem=sent.at[turn, part],
+                recv_sem=came.at[turn, part],
+                device_id=(to_e, to_p),
+                device_id_type=MESH,
+            ).start()
+
+        peers(start)
+
+    def arrive(source, target, turn, part):
+        stay = pltpu.make_async_copy(source.at[me], target.at[me], kept)
         stay.start()
         stay.wait()
-        pltpu.make_async_copy(target.at[others], target.at[others], came.at[turn]).wait()
-
-    fetches[1].wait()
-    fetches[2].wait()
-    value = jnp.concatenate([less[0], greater[0], less[1], greater[1]], axis=0)
-    for to_core in (1, 0):
-        half = SLOTS // 2
-        ordered = dot(hot[(1 - to_core) * half : (2 - to_core) * half, :], value, ((1,), (1,)))
-        parts = [ordered[:, part * 128 : (part + 1) * 128].reshape(EDEV, MINE, 128) for part in range(2)]
-        send_one[(1 - to_core) * EDEV : (2 - to_core) * EDEV] = jnp.concatenate(parts, axis=1).astype(BF16)
-        if to_core == 1:
+        pltpu.make_async_copy(target.at[others], target.at[others], came.at[turn, part]).wait()
+
+    fetches[0].wait()
+    for part in range(ROUNDS):
+        hot = one_hot(slot[...], (part,))
+        if part == 0:
+            fetches[1].wait()
+            fetches[2].wait()
+        value = jnp.concatenate([less[0], greater[0], less[1], greater[1]], axis=0)
+        ordered = dot(hot, value, ((1,), (1,)))
+        for mine in range(MINE):
+            for half in range(2):
+                flat[pl.ds(half * MINE + mine, OWNERS, stride=ROWS), :] = ordered[
+                    mine * OWNERS : (mine + 1) * OWNERS, half * 128 : (half + 1) * 128
+                ]
+        send_one[part] = flat[...].reshape(OWNERS, ROWS, 128).astype(BF16)
+        if part == 0:
             pl.semaphore_wait(barrier, OWNERS - 1)
-        for odd in (1, 0):
-            some_peers(to_core, odd, out)
+        depart(send_one.at[part], recv_one.at[part], 0, part)
 
     fetches[3].wait()
     fetches[4].wait()
     coarse[...] = wide[...].astype(BF16)
-    arrive(send_one.at[owner], recv_one.at[place], recv_one, 0)
-    correlate(recv_one, send_two, coarse, fine, flat, y_own, y_far)
-    for to_core in (1, 0):
-        peers((to_core,), back)
-    arrive(send_two.at[place], recv_two.at[owner], recv_two, 1)
+    for part in range(ROUNDS):
+        arrive(send_one.at[part], recv_one.at[part], 0, part)
+        correlate(recv_one.at[part], send_two.at[part], coarse, fine, flat, y_own, y_far)
+        depart(send_two.at[part], recv_two.at[part], 1, part)
+    for part in range(ROUNDS):
+        arrive(send_two.at[part], recv_two.at[part], 1, part)
 
     for turn, source in enumerate((send_one, send_two)):
-        pltpu.make_async_copy(source.at[others], source.at[others], sent.at[turn]).wait()
-
-
-def reorder(back_hbm, slot_hbm, less_hbm, greater_hbm, back, slot, less, greater, fetched, stored):
+        for part in range(ROUNDS):
+            done = source.at[part].at[others]
+            pltpu.make_async_copy(done, done, sent.at[turn, part]).wait()
+
+
+def reorder(back_hbm, slot_hbm, less_hbm, greater_hbm, back, slot, flat, less, greater, fetched, stored):
     fetches = [
         pltpu.make_async_copy(slot_hbm, slot, fetched.at[0]),
         pltpu.make_async_copy(back_hbm, back, fetched.at[1]),
@@ -262,11 +247,18 @@
     for fetch in fetches:
         fetch.start()
     fetches[0].wait()
-    hot = one_hot(slot[...], 0, SLOTS)
+    hot = one_hot(slot[...], tuple(range(ROUNDS)))
     fetches[1].wait()
-    value = back[...].astype(F32)
+    count = ROUNDS * OWNERS
+    flat[...] = back[...].astype(F32).reshape(count * ROWS, 128)
     ordered = jnp.concatenate(
-        [value[:, part * MINE : (part + 1) * MINE].reshape(SLOTS, 128) for part in range(2)], axis=1
+        [
+            jnp.concatenate(
+                [flat[pl.ds(part * MINE + mine, count, stride=ROWS), :] for mine in range(MINE)], axis=0
+            )
+            for part in range(2)
+        ],
+        axis=1,
     )
     result = dot(ordered.astype(BF16), hot, ((0,), (0,))).astype(BF16)
     stores = []
@@ -283,10 +275,10 @@
     coarse, fine = tables()
     hbm = pl.BlockSpec(memory_space=pltpu.HBM)
     grant = 60 * 1024 * 1024
-    packets = pltpu.VMEM((OWNERS, ROWS, 128), BF16)
+    packets = pltpu.VMEM((ROUNDS, OWNERS, ROWS, 128), BF16)
     back = pl.pallas_call(
         kernel,
-        out_shape=jax.ShapeDtypeStruct((OWNERS, ROWS, 128), BF16),
+        out_shape=jax.ShapeDtypeStruct(packets.shape, BF16),
         in_specs=[hbm] * 5,
         out_specs=hbm,
         scratch_shapes=[
@@ -296,15 +288,14 @@
             pltpu.VMEM(coarse.shape, F32),
             pltpu.VMEM(coarse.shape, BF16),
             pltpu.VMEM(fine.shape, F32),
-            pltpu.VMEM((SLOTS, SLOTS), BF16),
             packets,
             packets,
             packets,
             pltpu.VMEM((OWNERS * ROWS, 128), F32),
             pltpu.VMEM((MINE * K0, 512), BF16),
             pltpu.VMEM((MINE * K0, 512), BF16),
-            pltpu.SemaphoreType.DMA((2,)),
-            pltpu.SemaphoreType.DMA((2,)),
+            pltpu.SemaphoreType.DMA((2, ROUNDS)),
+            pltpu.SemaphoreType.DMA((2, ROUNDS)),
             pltpu.SemaphoreType.DMA,
             pltpu.SemaphoreType.DMA((5,)),
         ],
@@ -320,6 +311,7 @@
         scratch_shapes=[
             packets,
             pltpu.VMEM((1, SLOTS), jnp.int32),
+            pltpu.VMEM((ROUNDS * OWNERS * ROWS, 128), F32),
             pltpu.VMEM(shape.shape, BF16),
             pltpu.VMEM(shape.shape, BF16),
             pltpu.SemaphoreType.DMA((2,)),

time: 68.7 us -> 69.6 us (1.013); the launches traced: 68.6 us -> 68.7 us
  no operation moved by 1% of the time
where the time goes in v6:
time: 69.6 us; the launch traced here: 68.7 us
  Pallas kernels  68.1 us (98%)
    pallas_call x1, Pallas kernels, per_device(): pl.pallas_call(kernel, out_shape=jax.ShapeDtypeStruct(packets.shape, BF16...  65.4 us
    pallas_call x1, Pallas kernels, per_device(): pl.pallas_call(reorder, out_shape=(shape, shape), in_specs=[hbm, hbm], ou...  2.73 us

profile of v6, /device:TPU:6, one launch (start us, length us, event | category | flops | bytes accessed | tf_op | source)
XLA Modules:
  0.0 68.7 jit_solution(3110972044811034091)
XLA Ops:
  0.6 65.4 %shard_map.68.back_hbm = bf16[2,128,8,128]{3,2,1,0:T(8,128)(2,1)} custom-call(bf16[2,64,1024]{2,1,0:T(8,128)(2,1)} %less_hbm.1, bf16[2,64,1024]{2,1,0:T(8,128)(2,1)} %greater_hbm.1, s32[1,1024]{1,0:T(1,128)} %slot_hbm.3, f32[20,128,256]{2,1,0:T(8,128)} %constant.4.clone.coarse_hbm, f32[4,128,128]{2,1,0:T(8,128)} %constant.5.clone.fine_hbm), custom_call_target="tpu_custom_call" | custom-call | flops 4000000000 | bytes 4000000 | tf_op jit(solution)/shard_map/pallas_call | solution.py:279
  66.0 2.7 %shard_map.69 = (bf16[2,64,1024]{2,1,0:T(8,128)(2,1)}, bf16[2,64,1024]{2,1,0:T(8,128)(2,1)}) custom-call(bf16[2,128,8,128]{3,2,1,0:T(8,128)(2,1)} %shard_map.68.back_hbm, s32[1,1024]{1,0:T(1,128)} %slot_hbm.3), custom_call_target="tpu_custom_call" | custom-call | flops 1000000000 | bytes 1000000 | tf_op jit(solution)/shard_map/pallas_call | solution.py:306

commit v7 on v4

--- a/solution.py
+++ b/solution.py
@@ -17,7 +17,7 @@
 SLOTS = 1024
 MINE = SLOTS // OWNERS
 ROWS = 2 * MINE
-EARLY_Z = 2
+EARLY_Z = 3
 K0 = 128
 K1 = 64
 LENGTH = 2 * NE
@@ -249,15 +249,18 @@
     coarse[...] = wide[...].astype(BF16)
     arrive(send_one.at[owner], recv_one.at[place], recv_one, 0)
     correlate(recv_one, send_two, coarse, fine, flat, y_own, y_far)
-    peers((1,), back)
-    for to_z in range(EARLY_Z):
-        at_z(to_z, 0, columns[1:], back)
-        pl.when(jnp.logical_or(z != to_z, core != 0))(functools.partial(at_z, to_z, 0, columns[:1], back))
+    def sooner(dz, to_core, columns, act):
+        to_z = jnp.where(z + dz >= 16, z + dz - 16, z + dz)
+        if to_core == 1:
+            at_z(to_z, to_core, columns, act)
+        else:
+            pl.when(to_z < EARLY_Z)(functools.partial(at_z, to_z, to_core, columns, act))
 
     def later(dz, to_core, columns, act):
         to_z = jnp.where(z + dz >= 16, z + dz - 16, z + dz)
         pl.when(to_z >= EARLY_Z)(functools.partial(at_z, to_z, to_core, columns, act))
 
+    peers((0, 1), back, sooner)
     peers((0,), back, later)
     arrive(send_two.at[place], recv_two.at[owner], recv_two, 1)
 

time: 68.1 us -> 67.9 us (level); the launches traced: 68 us -> 66.6 us
  Pallas kernels: 67.3 us -> 66 us
    pallas_call x1, Pallas kernels: 64.6 us -> 63.2 us  [per_device(): pl.pallas_call(kernel, out_shape=jax.ShapeDtypeStruct((OWNERS, ROWS, 128)...]
where the time goes in v7:
time: 67.9 us; the launch traced here: 66.6 us
  Pallas kernels  66 us (97%)
    pallas_call x1, Pallas kernels, per_device(): pl.pallas_call(kernel, out_shape=jax.ShapeDtypeStruct((OWNERS, ROWS, 128)...  63.2 us
    pallas_call x1, Pallas kernels, per_device(): pl.pallas_call(reorder, out_shape=(shape, shape), in_specs=[hbm, hbm], ou...  2.78 us

profile of v7, /device:TPU:6, one launch (start us, length us, event | category | flops | bytes accessed | tf_op | source)
XLA Modules:
  0.0 66.6 jit_solution(11961161742011684055)
XLA Ops:
  0.6 63.2 %shard_map.68.back_hbm = bf16[128,16,128]{2,1,0:T(8,128)(2,1)} custom-call(bf16[2,64,1024]{2,1,0:T(8,128)(2,1)} %less_hbm.1, bf16[2,64,1024]{2,1,0:T(8,128)(2,1)} %greater_hbm.1, s32[1,1024]{1,0:T(1,128)} %slot_hbm.3, f32[20,128,256]{2,1,0:T(8,128)} %constant.4.clone.coarse_hbm, f32[4,128,128]{2,1,0:T(8,128)} %constant.5.clone.fine_hbm), custom_call_target="tpu_custom_call" | custom-call | flops 4000000000 | bytes 4000000 | tf_op jit(solution)/shard_map/pallas_call | solution.py:301
  63.8 2.8 %shard_map.69 = (bf16[2,64,1024]{2,1,0:T(8,128)(2,1)}, bf16[2,64,1024]{2,1,0:T(8,128)(2,1)}) custom-call(bf16[128,16,128]{2,1,0:T(8,128)(2,1)} %shard_map.68.back_hbm, s32[1,1024]{1,0:T(1,128)} %slot_hbm.3), custom_call_target="tpu_custom_call" | custom-call | flops 1000000000 | bytes 1000000 | tf_op jit(solution)/shard_map/pallas_call | solution.py:329

commit v8 on v4

--- a/solution.py
+++ b/solution.py
@@ -135,7 +135,7 @@
     recv_two,
     less, greater, slot, wide, coarse, fine,
     hot, send_one, recv_one, send_two, flat, y_own, y_far,
-    sent, came, kept, fetched,
+    my_turn, left_far, left_near, sent, came, kept, fetched,
 ):
     e = lax.axis_index("energy")
     p = lax.axis_index("pair")
@@ -183,20 +183,24 @@
             visit(0, to_core, columns[1:], act)
             pl.when(core != to_core)(functools.partial(visit, 0, to_core, columns[:1], act))
 
-    def some_peers(to_core, odd, act):
-        even = 1 - lax.rem(odd + z, 2)
-
+    def far_peers(to_core, act):
         def both_ways(near, carry):
-            at(7 + even - 2 * near, to_core, columns, act)
-            at(9 + even + 2 * near, to_core, columns, act)
+            at(7 - near, to_core, columns, act)
+            at(9 + near, to_core, columns, act)
             return carry
 
+        at(8, to_core, columns, act)
+        lax.fori_loop(0, 4, both_ways, 0)
+
+    def near_peers(to_core, act):
+        def both_ways(near, carry):
+            at(3 - near, to_core, columns, act)
+            at(13 + near, to_core, columns, act)
+            return carry
+
         lax.fori_loop(0, 3, both_ways, 0)
-        at(1 + even, to_core, columns, act)
-        at(15 + even, to_core, columns[1:], act)
-        pl.when(jnp.logical_or(even == 0, core != to_core))(
-            functools.partial(at, 15 + even, to_core, columns[:1], act)
-        )
+        at(0, to_core, columns[1:], act)
+        pl.when(core != to_core)(functools.partial(at, 0, to_core, columns[:1], act))
 
     barrier = pltpu.get_barrier_semaphore()
 
@@ -207,21 +211,23 @@
     fetches[0].wait()
     hot[...] = one_hot(slot[...], 0, SLOTS)
 
-    def remote(src, dst, turn, to_e, to_p):
+    def remote(src, dst, departure, arrival, to_e, to_p):
         pltpu.make_async_remote_copy(
             src_ref=src,
             dst_ref=dst,
-            send_sem=sent.at[turn],
-            recv_sem=came.at[turn],
+            send_sem=departure,
+            recv_sem=arrival,
             device_id=(to_e, to_p),
             device_id_type=MESH,
         ).start()
 
-    def out(to_e, to_p, to_place, to_owner):
-        remote(send_one.at[to_owner], recv_one.at[place], 0, to_e, to_p)
+    def out(departure):
+        return lambda to_e, to_p, to_place, to_owner: remote(
+            send_one.at[to_owner], recv_one.at[place], departure, came.at[0], to_e, to_p
+        )
 
     def back(to_e, to_p, to_place, to_owner):
-        remote(send_two.at[to_place], recv_two.at[owner], 1, to_e, to_p)
+        remote(send_two.at[to_place], recv_two.at[owner], sent, came.at[1], to_e, to_p)
 
     others = pl.ds(0, OWNERS - 1)
 
@@ -234,15 +240,33 @@
     fetches[1].wait()
     fetches[2].wait()
     value = jnp.concatenate([less[0], greater[0], less[1], greater[1]], axis=0)
-    for to_core in (1, 0):
+
+    def permute(to_core):
         half = SLOTS // 2
         ordered = dot(hot[(1 - to_core) * half : (2 - to_core) * half, :], value, ((1,), (1,)))
         parts = [ordered[:, part * 128 : (part + 1) * 128].reshape(EDEV, MINE, 128) for part in range(2)]
         send_one[(1 - to_core) * EDEV : (2 - to_core) * EDEV] = jnp.concatenate(parts, axis=1).astype(BF16)
-        if to_core == 1:
-            pl.semaphore_wait(barrier, OWNERS - 1)
-        for odd in (1, 0):
-            some_peers(to_core, odd, out)
+
+    def hand_over(to_core):
+        far = pl.ds(0, 36)
+        pltpu.make_async_copy(send_one.at[far], send_one.at[far], left_far.at[to_core]).wait()
+        sibling = e + 1 - 2 * core
+        pl.semaphore_signal(my_turn, inc=1, device_id=(sibling, p), device_id_type=MESH)
+
+    def take_over():
+        pl.semaphore_wait(my_turn, 1)
+
+    permute(1)
+    pl.semaphore_wait(barrier, OWNERS - 1)
+    pl.when(core == 0)(take_over)
+    far_peers(1, out(left_far.at[1]))
+    near_peers(1, out(left_near.at[1]))
+    permute(0)
+    hand_over(1)
+    take_over()
+    far_peers(0, out(left_far.at[0]))
+    near_peers(0, out(left_near.at[0]))
+    pl.when(core == 1)(functools.partial(hand_over, 0))
 
     fetches[3].wait()
     fetches[4].wait()
@@ -261,8 +285,15 @@
     peers((0,), back, later)
     arrive(send_two.at[place], recv_two.at[owner], recv_two, 1)
 
-    for turn, source in enumerate((send_one, send_two)):
-        pltpu.make_async_copy(source.at[others], source.at[others], sent.at[turn]).wait()
+    def drain(source, count, departure):
+        some = source.at[pl.ds(0, count)]
+        pltpu.make_async_copy(some, some, departure).wait()
+
+    pl.when(core == 0)(functools.partial(drain, send_one, 36, left_far.at[0]))
+    for to_core in (1, 0):
+        pl.when(core == to_core)(functools.partial(drain, send_one, 27, left_near.at[to_core]))
+        pl.when(core != to_core)(functools.partial(drain, send_one, 28, left_near.at[to_core]))
+    drain(send_two, OWNERS - 1, sent)
 
 
 def reorder(back_hbm, slot_hbm, less_hbm, greater_hbm, back, slot, less, greater, fetched, stored):
@@ -314,7 +345,10 @@
             pltpu.VMEM((OWNERS * ROWS, 128), F32),
             pltpu.VMEM((MINE * K0, 512), BF16),
             pltpu.VMEM((MINE * K0, 512), BF16),
+            pltpu.SemaphoreType.REGULAR,
             pltpu.SemaphoreType.DMA((2,)),
+            pltpu.SemaphoreType.DMA((2,)),
+            pltpu.SemaphoreType.DMA,
             pltpu.SemaphoreType.DMA((2,)),
             pltpu.SemaphoreType.DMA,
             pltpu.SemaphoreType.DMA((5,)),

time: 68.1 us -> 68.3 us (level); the launches traced: 68 us -> 67.4 us
  no operation moved by 1% of the time
where the time goes in v8:
time: 68.3 us; the launch traced here: 67.4 us
  Pallas kernels  66.7 us (98%)
    pallas_call x1, Pallas kernels, per_device(): pl.pallas_call(kernel, out_shape=jax.ShapeDtypeStruct((OWNERS, ROWS, 128)...  64 us
    pallas_call x1, Pallas kernels, per_device(): pl.pallas_call(reorder, out_shape=(shape, shape), in_specs=[hbm, hbm], ou...  2.77 us

profile of v8, /device:TPU:6, one launch (start us, length us, event | category | flops | bytes accessed | tf_op | source)
XLA Modules:
  0.0 67.4 jit_solution(4330153061572679955)
XLA Ops:
  0.6 64.0 %shard_map.68.back_hbm = bf16[128,16,128]{2,1,0:T(8,128)(2,1)} custom-call(bf16[2,64,1024]{2,1,0:T(8,128)(2,1)} %less_hbm.1, bf16[2,64,1024]{2,1,0:T(8,128)(2,1)} %greater_hbm.1, s32[1,1024]{1,0:T(1,128)} %slot_hbm.3, f32[20,128,256]{2,1,0:T(8,128)} %constant.4.clone.coarse_hbm, f32[4,128,128]{2,1,0:T(8,128)} %constant.5.clone.fine_hbm), custom_call_target="tpu_custom_call" | custom-call | flops 4000000000 | bytes 4000000 | tf_op jit(solution)/shard_map/pallas_call | solution.py:329
  64.6 2.8 %shard_map.69 = (bf16[2,64,1024]{2,1,0:T(8,128)(2,1)}, bf16[2,64,1024]{2,1,0:T(8,128)(2,1)}) custom-call(bf16[128,16,128]{2,1,0:T(8,128)(2,1)} %shard_map.68.back_hbm, s32[1,1024]{1,0:T(1,128)} %slot_hbm.3), custom_call_target="tpu_custom_call" | custom-call | flops 1000000000 | bytes 1000000 | tf_op jit(solution)/shard_map/pallas_call | solution.py:360

commit v9 on v4

--- a/solution.py
+++ b/solution.py
@@ -145,12 +145,6 @@
     place = e * 2 + side
     owner = (1 - core) * EDEV + lax.div(e, 2) * 2 + side
 
-    sources = (slot_hbm, less_hbm, greater_hbm, coarse_hbm, fine_hbm)
-    places = (slot, less, greater, wide, fine)
-    fetches = [pltpu.make_async_copy(a, b, fetched.at[i]) for i, (a, b) in enumerate(zip(sources, places))]
-    for fetch in fetches:
-        fetch.start()
-
     columns = []
     for dy in range(4):
         to_y = lax.rem(y + dy, 4)
@@ -204,6 +198,12 @@
         pl.semaphore_signal(barrier, inc=1, device_id=(to_e, to_p), device_id_type=MESH)
 
     peers((1, 0), greet)
+
+    sources = (slot_hbm, less_hbm, greater_hbm, coarse_hbm, fine_hbm)
+    places = (slot, less, greater, wide, fine)
+    fetches = [pltpu.make_async_copy(a, b, fetched.at[i]) for i, (a, b) in enumerate(zip(sources, places))]
+    for fetch in fetches:
+        fetch.start()
     fetches[0].wait()
     hot[...] = one_hot(slot[...], 0, SLOTS)
 
@@ -273,13 +273,19 @@
     for fetch in fetches:
         fetch.start()
     fetches[0].wait()
-    hot = one_hot(slot[...], 0, SLOTS)
+    half = SLOTS // 2
+    hot = one_hot(slot[...], 0, half)
     fetches[1].wait()
-    value = back[...].astype(F32)
-    ordered = jnp.concatenate(
-        [value[:, part * MINE : (part + 1) * MINE].reshape(SLOTS, 128) for part in range(2)], axis=1
-    )
-    result = dot(ordered.astype(BF16), hot, ((0,), (0,))).astype(BF16)
+    result = None
+    for part in range(2):
+        value = back[part * EDEV : (part + 1) * EDEV].astype(F32)
+        ordered = jnp.concatenate([value[:, :MINE].reshape(half, 128), value[:, MINE:].reshape(half, 128)], axis=1)
+        term = dot(ordered.astype(BF16), hot, ((0,), (0,)))
+        if part == 0:
+            hot = one_hot(slot[...], half, half)
+            result = term
+        else:
+            result = (result + term).astype(BF16)
     stores = []
     for part in range(2):
         for array, (kept, result_hbm) in enumerate(((less, less_hbm), (greater, greater_hbm))):

time: 68.1 us -> 68 us (level)
  no operation moved by 1% of the time
where the time goes in v9:
time: 68 us; the launch traced here: 67.8 us
  Pallas kernels  67.2 us (99%)
    pallas_call x1, Pallas kernels, per_device(): pl.pallas_call(kernel, out_shape=jax.ShapeDtypeStruct((OWNERS, ROWS, 128)...  64.6 us
    pallas_call x1, Pallas kernels, per_device(): pl.pallas_call(reorder, out_shape=(shape, shape), in_specs=[hbm, hbm], ou...  2.59 us

profile of v9, /device:TPU:6, one launch (start us, length us, event | category | flops | bytes accessed | tf_op | source)
XLA Modules:
  0.0 67.8 jit_solution(15352829485020474507)
XLA Ops:
  0.6 64.6 %shard_map.68.back_hbm = bf16[128,16,128]{2,1,0:T(8,128)(2,1)} custom-call(bf16[2,64,1024]{2,1,0:T(8,128)(2,1)} %less_hbm.1, bf16[2,64,1024]{2,1,0:T(8,128)(2,1)} %greater_hbm.1, s32[1,1024]{1,0:T(1,128)} %slot_hbm.3, f32[20,128,256]{2,1,0:T(8,128)} %constant.4.clone.coarse_hbm, f32[4,128,128]{2,1,0:T(8,128)} %constant.5.clone.fine_hbm), custom_call_target="tpu_custom_call" | custom-call | flops 4000000000 | bytes 4000000 | tf_op jit(solution)/shard_map/pallas_call | solution.py:304
  65.2 2.6 %shard_map.69 = (bf16[2,64,1024]{2,1,0:T(8,128)(2,1)}, bf16[2,64,1024]{2,1,0:T(8,128)(2,1)}) custom-call(bf16[128,16,128]{2,1,0:T(8,128)(2,1)} %shard_map.68.back_hbm, s32[1,1024]{1,0:T(1,128)} %slot_hbm.3), custom_call_target="tpu_custom_call" | custom-call | flops 1000000000 | bytes 1000000 | tf_op jit(solution)/shard_map/pallas_call | solution.py:332

commit v10 on v9

--- a/solution.py
+++ b/solution.py
@@ -17,7 +17,7 @@
 SLOTS = 1024
 MINE = SLOTS // OWNERS
 ROWS = 2 * MINE
-EARLY_Z = 2
+EARLY_Z = 4
 K0 = 128
 K1 = 64
 LENGTH = 2 * NE
@@ -249,16 +249,17 @@
     coarse[...] = wide[...].astype(BF16)
     arrive(send_one.at[owner], recv_one.at[place], recv_one, 0)
     correlate(recv_one, send_two, coarse, fine, flat, y_own, y_far)
-    peers((1,), back)
-    for to_z in range(EARLY_Z):
-        at_z(to_z, 0, columns[1:], back)
-        pl.when(jnp.logical_or(z != to_z, core != 0))(functools.partial(at_z, to_z, 0, columns[:1], back))
-
-    def later(dz, to_core, columns, act):
+    def lowest(dz, to_core, columns, act):
+        to_z = jnp.where(z + dz >= 16, z + dz - 16, z + dz)
+        pl.when(to_z < EARLY_Z)(functools.partial(at_z, to_z, to_core, columns, act))
+
+    def rest(dz, to_core, columns, act):
         to_z = jnp.where(z + dz >= 16, z + dz - 16, z + dz)
         pl.when(to_z >= EARLY_Z)(functools.partial(at_z, to_z, to_core, columns, act))
 
-    peers((0,), back, later)
+    peers((1,), back)
+    peers((0,), back, lowest)
+    peers((0,), back, rest)
     arrive(send_two.at[place], recv_two.at[owner], recv_two, 1)
 
     for turn, source in enumerate((send_one, send_two)):

time: 68 us -> 68 us (level)
  no operation moved by 1% of the time
where the time goes in v10:
time: 68 us; the launch traced here: 67.9 us
  Pallas kernels  67.2 us (99%)
    pallas_call x1, Pallas kernels, per_device(): pl.pallas_call(kernel, out_shape=jax.ShapeDtypeStruct((OWNERS, ROWS, 128)...  64.6 us
    pallas_call x1, Pallas kernels, per_device(): pl.pallas_call(reorder, out_shape=(shape, shape), in_specs=[hbm, hbm], ou...  2.59 us

profile of v10, /device:TPU:6, one launch (start us, length us, event | category | flops | bytes accessed | tf_op | source)
XLA Modules:
  0.0 67.9 jit_solution(2203856808592812029)
XLA Ops:
  0.6 64.6 %shard_map.68.back_hbm = bf16[128,16,128]{2,1,0:T(8,128)(2,1)} custom-call(bf16[2,64,1024]{2,1,0:T(8,128)(2,1)} %less_hbm.1, bf16[2,64,1024]{2,1,0:T(8,128)(2,1)} %greater_hbm.1, s32[1,1024]{1,0:T(1,128)} %slot_hbm.3, f32[20,128,256]{2,1,0:T(8,128)} %constant.4.clone.coarse_hbm, f32[4,128,128]{2,1,0:T(8,128)} %constant.5.clone.fine_hbm), custom_call_target="tpu_custom_call" | custom-call | flops 4000000000 | bytes 4000000 | tf_op jit(solution)/shard_map/pallas_call | solution.py:305
  65.3 2.6 %shard_map.69 = (bf16[2,64,1024]{2,1,0:T(8,128)(2,1)}, bf16[2,64,1024]{2,1,0:T(8,128)(2,1)}) custom-call(bf16[128,16,128]{2,1,0:T(8,128)(2,1)} %shard_map.68.back_hbm, s32[1,1024]{1,0:T(1,128)} %slot_hbm.3), custom_call_target="tpu_custom_call" | custom-call | flops 1000000000 | bytes 1000000 | tf_op jit(solution)/shard_map/pallas_call | solution.py:333

commit v11 on v9

--- a/solution.py
+++ b/solution.py
@@ -98,7 +98,7 @@
             jnp.concatenate([value, value[:, :256]], axis=1), jnp.concatenate([upper, upper, lower], axis=0)
         )
 
-    group = 4
+    group = MINE
     for step in range(MINE // group):
         rows = pl.ds(step * (group * K0), group * K0)
         left, right = triple(y_own[rows, :], own), triple(y_far[rows, :], far)

time: 68 us -> 67.8 us (level)
  no operation moved by 1% of the time
where the time goes in v11:
time: 67.8 us; the launch traced here: 67.7 us
  Pallas kernels  67 us (99%)
    pallas_call x1, Pallas kernels, per_device(): pl.pallas_call(kernel, out_shape=jax.ShapeDtypeStruct((OWNERS, ROWS, 128)...  64.4 us
    pallas_call x1, Pallas kernels, per_device(): pl.pallas_call(reorder, out_shape=(shape, shape), in_specs=[hbm, hbm], ou...  2.59 us

profile of v11, /device:TPU:6, one launch (start us, length us, event | category | flops | bytes accessed | tf_op | source)
XLA Modules:
  0.0 67.7 jit_solution(1095641816760431371)
XLA Ops:
  0.6 64.4 %shard_map.68.back_hbm = bf16[128,16,128]{2,1,0:T(8,128)(2,1)} custom-call(bf16[2,64,1024]{2,1,0:T(8,128)(2,1)} %less_hbm.1, bf16[2,64,1024]{2,1,0:T(8,128)(2,1)} %greater_hbm.1, s32[1,1024]{1,0:T(1,128)} %slot_hbm.3, f32[20,128,256]{2,1,0:T(8,128)} %constant.4.clone.coarse_hbm, f32[4,128,128]{2,1,0:T(8,128)} %constant.5.clone.fine_hbm), custom_call_target="tpu_custom_call" | custom-call | flops 4000000000 | bytes 4000000 | tf_op jit(solution)/shard_map/pallas_call | solution.py:304
  65.1 2.6 %shard_map.69 = (bf16[2,64,1024]{2,1,0:T(8,128)(2,1)}, bf16[2,64,1024]{2,1,0:T(8,128)(2,1)}) custom-call(bf16[128,16,128]{2,1,0:T(8,128)(2,1)} %shard_map.68.back_hbm, s32[1,1024]{1,0:T(1,128)} %slot_hbm.3), custom_call_target="tpu_custom_call" | custom-call | flops 1000000000 | bytes 1000000 | tf_op jit(solution)/shard_map/pallas_call | solution.py:332

commit v12 on v11

--- a/solution.py
+++ b/solution.py
@@ -134,7 +134,7 @@
     less_hbm, greater_hbm, slot_hbm, coarse_hbm, fine_hbm,
     recv_two,
     less, greater, slot, wide, coarse, fine,
-    hot, send_one, recv_one, send_two, flat, y_own, y_far,
+    send_one, recv_one, send_two, flat, y_own, y_far,
     sent, came, kept, fetched,
 ):
     e = lax.axis_index("energy")
@@ -146,7 +146,7 @@
     owner = (1 - core) * EDEV + lax.div(e, 2) * 2 + side
 
     columns = []
-    for dy in range(4):
+    for dy in (0, 2, 1, 3):
         to_y = lax.rem(y + dy, 4)
         columns.append((lax.div(to_y, 2) * 16, lax.rem(to_y, 2)))
 
@@ -205,7 +205,6 @@
     for fetch in fetches:
         fetch.start()
     fetches[0].wait()
-    hot[...] = one_hot(slot[...], 0, SLOTS)
 
     def remote(src, dst, turn, to_e, to_p):
         pltpu.make_async_remote_copy(
@@ -236,7 +235,7 @@
     value = jnp.concatenate([less[0], greater[0], less[1], greater[1]], axis=0)
     for to_core in (1, 0):
         half = SLOTS // 2
-        ordered = dot(hot[(1 - to_core) * half : (2 - to_core) * half, :], value, ((1,), (1,)))
+        ordered = dot(one_hot(slot[...], (1 - to_core) * half, half), value, ((1,), (1,)))
         parts = [ordered[:, part * 128 : (part + 1) * 128].reshape(EDEV, MINE, 128) for part in range(2)]
         send_one[(1 - to_core) * EDEV : (2 - to_core) * EDEV] = jnp.concatenate(parts, axis=1).astype(BF16)
         if to_core == 1:
@@ -313,7 +312,6 @@
             pltpu.VMEM(coarse.shape, F32),
             pltpu.VMEM(coarse.shape, BF16),
             pltpu.VMEM(fine.shape, F32),
-            pltpu.VMEM((SLOTS, SLOTS), BF16),
             packets,
             packets,
             packets,

time: 67.8 us -> 67.7 us (level)
  no operation moved by 1% of the time
where the time goes in v12:
time: 67.7 us; the launch traced here: 67.6 us
  Pallas kernels  66.9 us (99%)
    pallas_call x1, Pallas kernels, per_device(): pl.pallas_call(kernel, out_shape=jax.ShapeDtypeStruct((OWNERS, ROWS, 128)...  64.3 us
    pallas_call x1, Pallas kernels, per_device(): pl.pallas_call(reorder, out_shape=(shape, shape), in_specs=[hbm, hbm], ou...  2.59 us

profile of v12, /device:TPU:6, one launch (start us, length us, event | category | flops | bytes accessed | tf_op | source)
XLA Modules:
  0.0 67.6 jit_solution(18145704054048356118)
XLA Ops:
  0.6 64.3 %shard_map.68.back_hbm = bf16[128,16,128]{2,1,0:T(8,128)(2,1)} custom-call(bf16[2,64,1024]{2,1,0:T(8,128)(2,1)} %less_hbm.1, bf16[2,64,1024]{2,1,0:T(8,128)(2,1)} %greater_hbm.1, s32[1,1024]{1,0:T(1,128)} %slot_hbm.3, f32[20,128,256]{2,1,0:T(8,128)} %constant.4.clone.coarse_hbm, f32[4,128,128]{2,1,0:T(8,128)} %constant.5.clone.fine_hbm), custom_call_target="tpu_custom_call" | custom-call | flops 4000000000 | bytes 4000000 | tf_op jit(solution)/shard_map/pallas_call | solution.py:303
  65.0 2.6 %shard_map.69 = (bf16[2,64,1024]{2,1,0:T(8,128)(2,1)}, bf16[2,64,1024]{2,1,0:T(8,128)(2,1)}) custom-call(bf16[128,16,128]{2,1,0:T(8,128)(2,1)} %shard_map.68.back_hbm, s32[1,1024]{1,0:T(1,128)} %slot_hbm.3), custom_call_target="tpu_custom_call" | custom-call | flops 1000000000 | bytes 1000000 | tf_op jit(solution)/shard_map/pallas_call | solution.py:330

commit v13 on v12

--- a/solution.py
+++ b/solution.py
@@ -17,7 +17,7 @@
 SLOTS = 1024
 MINE = SLOTS // OWNERS
 ROWS = 2 * MINE
-EARLY_Z = 2
+EARLY_Z = 3
 K0 = 128
 K1 = 64
 LENGTH = 2 * NE

time: 67.7 us -> 67.8 us (level)
  no operation moved by 1% of the time
where the time goes in v13:
time: 67.8 us; the launch traced here: 67.6 us
  Pallas kernels  67 us (99%)
    pallas_call x1, Pallas kernels, per_device(): pl.pallas_call(kernel, out_shape=jax.ShapeDtypeStruct((OWNERS, ROWS, 128)...  64.4 us
    pallas_call x1, Pallas kernels, per_device(): pl.pallas_call(reorder, out_shape=(shape, shape), in_specs=[hbm, hbm], ou...  2.59 us

profile of v13, /device:TPU:6, one launch (start us, length us, event | category | flops | bytes accessed | tf_op | source)
XLA Modules:
  0.0 67.6 jit_solution(110688554851848389)
XLA Ops:
  0.6 64.4 %shard_map.68.back_hbm = bf16[128,16,128]{2,1,0:T(8,128)(2,1)} custom-call(bf16[2,64,1024]{2,1,0:T(8,128)(2,1)} %less_hbm.1, bf16[2,64,1024]{2,1,0:T(8,128)(2,1)} %greater_hbm.1, s32[1,1024]{1,0:T(1,128)} %slot_hbm.3, f32[20,128,256]{2,1,0:T(8,128)} %constant.4.clone.coarse_hbm, f32[4,128,128]{2,1,0:T(8,128)} %constant.5.clone.fine_hbm), custom_call_target="tpu_custom_call" | custom-call | flops 4000000000 | bytes 4000000 | tf_op jit(solution)/shard_map/pallas_call | solution.py:303
  65.0 2.6 %shard_map.69 = (bf16[2,64,1024]{2,1,0:T(8,128)(2,1)}, bf16[2,64,1024]{2,1,0:T(8,128)(2,1)}) custom-call(bf16[128,16,128]{2,1,0:T(8,128)(2,1)} %shard_map.68.back_hbm, s32[1,1024]{1,0:T(1,128)} %slot_hbm.3), custom_call_target="tpu_custom_call" | custom-call | flops 1000000000 | bytes 1000000 | tf_op jit(solution)/shard_map/pallas_call | solution.py:330
